TPU v7x, 32 devices: a whole 2x2x4 slice. The times are simulated.
32 devices in a mesh: ctx: 4 (over z), enc: 4 (over y, core), mp: 2 (over x).
Axes of the slice: x: 2, y: 2, z: 4, core: 2. Of those that a mesh axis runs over, the one named last changes fastest.
Arguments:
- hidden_in: bfloat16 [1024, 4096], P('ctx'), may hold values from -6 to 6
- norm_gains: float32 [2, 4096], replicated, may hold values from 0.5 to 1.5
- w_cross_query: bfloat16 [4096, 2048], P('ctx', ('enc', 'mp')), may hold values from -1 to 1
- w_cross_out: bfloat16 [2048, 4096], P(('enc', 'mp'), 'ctx'), may hold values from -0.125 to 0.125
- w_self_qkv: bfloat16 [4096, 3, 2048], P('ctx', None, ('enc', 'mp')), may hold values from -1 to 1
- w_self_out: bfloat16 [2048, 4096], P(('enc', 'mp'), 'ctx'), may hold values from -0.125 to 0.125
- nbr_kv: bfloat16 [4, 4, 4, 3, 64, 1024], P('ctx', 'enc', None, None, None, 'mp'), may hold values from -6 to 6
- nbr_count: int32 [16], P('ctx'), may hold values from 1 to 2
- nbr_source: int32 [16, 2], P('ctx'), may hold values from 0 to 3, all different within a row; in each aligned block of 4 rows (0 to 3, 4 to 7, ...) at most 3 rows name the same one
- span_order: int32 [16], replicated, may hold values from 0 to 15, each once
Outputs:
- block_out: bfloat16 [1024, 4096], P('ctx', ('enc', 'mp'))
Inputs may be any that keep to these rules, and one draw needn't show every extreme that they name: `nbr_source`: within the 4 stored spans of one index of ctx (aligned blocks of rows), no encoder index is named more than 3 times, and one is named exactly 3 times in some block; the 2 entries of a span differ. `span_order`: each of the 16 positions appears once.
All inputs are finite; a program needn't handle non-finite values.
Results may differ from a plain program's by a relative error of at most 0.015.
Values may be sent and summed in bfloat16 or wider, within the bound.
A program may use at most 128 MiB of HBM per device.

v0:
```python
import math

import jax
import jax.numpy as jnp
from jax import lax
from jax.sharding import PartitionSpec as P

HD = 128
SPAN = 64


epsilon = 1e-05
far_below = -1e30


def rms_rows(row_values, gain_row):
    values = row_values.astype(jnp.float32)
    row_scale = lax.rsqrt(jnp.mean(values * values, axis=-1, keepdims=True) + epsilon)
    return (values * row_scale * gain_row).astype(jnp.bfloat16)


def token_places(order_table, first_row, row_count):
    tokens = first_row + jnp.arange(row_count, dtype=jnp.int32)
    blocks = tokens // SPAN
    matches = blocks[:, None] == jnp.arange(order_table.shape[0], dtype=jnp.int32)[None, :]
    placed = jnp.sum(jnp.where(matches, order_table[None, :], 0), axis=1)
    return placed * SPAN + tokens % SPAN


def per_device(
    hidden_in,
    norm_gains,
    w_cross_query,
    w_cross_out,
    w_self_qkv,
    w_self_out,
    nbr_kv,
    nbr_count,
    nbr_source,
    span_order,
):
    tok_rows, model_width = hidden_in.shape
    features = w_cross_query.shape[1]
    heads_here = features // HD
    groups = lax.axis_size(("enc", "mp"))
    share_width = model_width // groups
    group_index = lax.axis_index(("enc", "mp"))
    column = lax.axis_index("ctx")
    attn_scale = 1.0 / math.sqrt(HD)
    normed = rms_rows(hidden_in, norm_gains[0])
    columns_part = normed
    cross_query = jnp.dot(
        columns_part,
        lax.all_gather(w_cross_query, "ctx", axis=0, tiled=True),
        preferred_element_type=jnp.float32,
    ).astype(jnp.bfloat16)
    arrived = lax.all_to_all(nbr_kv[0, 0], "enc", split_axis=0, concat_axis=0, tiled=True)
    sources, slot_count, nbr_rows, pair_width = arrived.shape
    flattened = arrived.reshape(sources * slot_count, nbr_rows, pair_width)
    spans_here, per_span = nbr_source.shape
    chosen = nbr_source.reshape(-1)
    matches = (chosen[:, None] == jnp.arange(sources, dtype=jnp.int32)[None, :]).astype(jnp.int32)
    earlier = jnp.cumsum(matches, axis=0) - matches
    places = chosen * slot_count + jnp.sum(earlier * matches, axis=1)
    picked = jnp.take(flattened, places, axis=0)
    picked = picked.reshape(spans_here, per_span, nbr_rows, heads_here, 2, HD)
    nbr_keys = picked[:, :, :, :, 0, :]
    nbr_values = picked[:, :, :, :, 1, :]
    queries = cross_query.reshape(spans_here, tok_rows // spans_here, heads_here, HD)
    scores = (
        jnp.einsum("cqhd,cjrhd->chqjr", queries, nbr_keys, preferred_element_type=jnp.float32)
        * attn_scale
    )
    alive_mask = jnp.arange(per_span, dtype=jnp.int32)[None, :] < nbr_count[:, None]
    scores = jnp.where(alive_mask[:, None, None, :, None], scores, far_below)
    row_top = jnp.max(scores, axis=(3, 4), keepdims=True)
    weights_f = jnp.exp(scores - row_top)
    row_total = jnp.sum(weights_f, axis=(3, 4))
    mixed_heads = (
        jnp.einsum(
            "chqjr,cjrhd->chqd",
            weights_f.astype(jnp.bfloat16),
            nbr_values,
            preferred_element_type=jnp.float32,
        )
        / row_total[..., None]
    )
    cross_att = mixed_heads.transpose(0, 2, 1, 3).reshape(tok_rows, features).astype(jnp.bfloat16)
    cross_term = jnp.dot(
        cross_att,
        lax.all_gather(w_cross_out, "ctx", axis=1, tiled=True),
        preferred_element_type=jnp.float32,
    )
    summed = lax.psum(cross_term.astype(jnp.bfloat16), ("enc", "mp")).astype(jnp.float32)
    mid_full = (hidden_in.astype(jnp.float32) + summed).astype(jnp.bfloat16)
    mid_normed = rms_rows(mid_full, norm_gains[1])
    mid_share = lax.dynamic_slice_in_dim(mid_full, group_index * share_width, share_width, 1)
    shard_piece = lax.all_gather(w_self_qkv, "ctx", axis=0, tiled=True)
    columns_part = mid_normed
    projected = jnp.dot(
        columns_part,
        shard_piece.reshape(shard_piece.shape[0], 3 * features),
        preferred_element_type=jnp.float32,
    )
    projected = projected.astype(jnp.bfloat16).reshape(tok_rows, 3, heads_here, HD)
    self_query = projected[:, 0]
    keys_values = projected[:, 1:]
    query_places = token_places(span_order, column * tok_rows, tok_rows)
    shard_piece = lax.all_gather(keys_values, "ctx", axis=0, tiled=True)
    old_top = jnp.full((heads_here, tok_rows), far_below, jnp.float32)
    key_places = token_places(span_order, jnp.int32(0), shard_piece.shape[0])
    block_scores = (
        jnp.einsum(
            "qhd,khd->hqk", self_query, shard_piece[:, 0], preferred_element_type=jnp.float32
        )
        * attn_scale
    )
    visible = key_places[None, None, :] <= query_places[None, :, None]
    block_scores = jnp.where(visible, block_scores, far_below)
    new_top = jnp.maximum(old_top, jnp.max(block_scores, axis=2))
    block_weights = jnp.where(visible, jnp.exp(block_scores - new_top[..., None]), 0.0)
    new_total = jnp.sum(block_weights, axis=2)
    running = jnp.einsum(
        "hqk,khd->hqd",
        block_weights.astype(jnp.bfloat16),
        shard_piece[:, 1],
        preferred_element_type=jnp.float32,
    )
    self_att = (
        (running / new_total[..., None])
        .transpose(1, 0, 2)
        .reshape(tok_rows, features)
        .astype(jnp.bfloat16)
    )
    self_term = jnp.dot(
        self_att,
        lax.all_gather(w_self_out, "ctx", axis=1, tiled=True),
        preferred_element_type=jnp.float32,
    )
    out_share = lax.psum_scatter(
        self_term.astype(jnp.bfloat16), ("enc", "mp"), scatter_dimension=1, tiled=True
    ).astype(jnp.float32)
    return (mid_share.astype(jnp.float32) + out_share).astype(jnp.bfloat16)


def solution(mesh):
    in_specs = (
        P("ctx", None),
        P(),
        P("ctx", ("enc", "mp")),
        P(("enc", "mp"), "ctx"),
        P("ctx", None, ("enc", "mp")),
        P(("enc", "mp"), "ctx"),
        P("ctx", "enc", None, None, None, "mp"),
        P("ctx"),
        P("ctx", None),
        P(),
    )
    out_specs = P("ctx", ("enc", "mp"))
    return jax.shard_map(
        per_device, mesh=mesh, in_specs=in_specs, out_specs=out_specs, check_vma=False
    )
```

profile of v0, /device:TPU:0, one launch (start us, length us, event | category | flops | bytes accessed | tf_op | source)
XLA Modules:
  0.0 415.8 jit_solution(16578737319240358672)
XLA Ops:
  6.5 0.7 all-gather.6.cloned.1.call-update
  7.3 4.2 %all-to-all-start = ((bf16[4,3,64,512]{3,2,1,0:T(8,128)(2,1)}), bf16[4,3,64,512]{3,2,1,0:T(8,128)(2,1)S(1)}, u32[]{:S(2)}, u32[]{:S(2)}) async-start(bf16[4,3,64,512]{3,2,1,0:T(8,128)(2,1)} %bitcast.71), calls=%async_computation | async-start | bytes 1572864 | tf_op jit(solution)/shard_map/all_to_all | solution.py:57
  11.5 0.7 all-gather.8.cloned.1.call-update
  12.3 0.0 all-reduce.2.cloned.1.call-start
  12.3 0.1 copy.28
  12.4 0.1 reshape.199
  12.5 0.2 reduce_window_sum.11
  12.7 0.1 mul.106
  12.8 0.1 reduce_sum.69
  12.9 0.1 iota_compare_fusion.3
  13.0 0.5 fusion.3
  13.5 9.6 %all-to-all-done = bf16[4,3,64,512]{3,2,1,0:T(8,128)(2,1)S(1)} async-done(((bf16[4,3,64,512]{3,2,1,0:T(8,128)(2,1)}), bf16[4,3,64,512]{3,2,1,0:T(8,128)(2,1)S(1)}, u32[]{:S(2)}, u32[]{:S(2)}) %all-to-all-start) | async-done | bytes 786464 | tf_op jit(solution)/shard_map/all_to_all | solution.py:57
  23.2 0.6 gather_fusion
  23.8 0.1 gather.7
  23.9 0.1 copy_select_fusion
  24.0 33.6 %all-gather.6.cloned.1.call-done = bf16[4096,256]{1,0:T(8,128)(2,1)} async-done(((bf16[1024,256]{1,0:T(8,128)(2,1)}), bf16[4096,256]{1,0:T(8,128)(2,1)}) %all-gather.6.cloned.1.call-update) | async-done | bytes 2097168 | tf_op jit(solution)/shard_map/all_gather | solution.py:54
  57.6 2.4 fusion.23
  60.0 0.2 fusion.34
  60.3 0.2 fusion.35
  60.5 0.4 fusion.27
  60.8 0.1 copy.33
  61.0 42.9 %all-gather.8.cloned.1.call-done = bf16[256,4096]{1,0:T(8,128)(2,1)} async-done(((bf16[256,1024]{1,0:T(8,128)(2,1)}), bf16[256,4096]{1,0:T(8,128)(2,1)}) %all-gather.8.cloned.1.call-update) | async-done | bytes 2097168 | tf_op jit(solution)/shard_map/all_gather | solution.py:91
  103.9 3.6 convolution_convert_fusion.1
  107.5 0.0 all-gather.10.cloned.1.call-start
  107.6 2.6 copy.34
  110.2 0.0 all-gather.12.cloned.1.call-start
  110.2 57.6 %all-reduce.2.cloned.1.call-done = bf16[256,4096]{1,0:T(8,128)(2,1)} async-done(((bf16[256,4096]{1,0:T(8,128)(2,1)}), bf16[256,4096]{1,0:T(8,128)(2,1)}) %all-reduce.2.cloned.1.call-update) | async-done | bytes 2097168 | tf_op jit(solution)/shard_map/psum | solution.py:94
  167.8 3.9 fusion
  171.7 112.1 %all-gather.10.cloned.1.call-done = bf16[4096,3,256]{0,2,1:T(8,128)(2,1)} async-done(((bf16[1024,3,256]{0,2,1:T(8,128)(2,1)}), bf16[4096,3,256]{0,2,1:T(8,128)(2,1)}) %all-gather.10.cloned.1.call-update) | async-done | bytes 6291472 | tf_op jit(solution)/shard_map/all_gather | solution.py:98
  283.9 5.3 %fusion.18 = bf16[256,768]{1,0:T(8,128)(2,1)S(1)} fusion(bf16[4096,768]{0,1:T(8,128)(2,1)} %bitcast.78, bf16[256,4096]{1,0:T(8,128)(2,1)} %get-tuple-element.6, f32[4096]{0:T(1024)S(1)} %bitcast.74, f32[256]{0:T(256)S(1)} %add_rsqrt_fusion), kind=kOutput, calls=%fused_computation.26 | convolution fusion | flops 1615003648 | bytes 8799232 | tf_op jit(solution)/shard_map/dot_general | solution.py:100
  289.2 0.1 reshape.202
  289.2 0.2 slice.37
  289.4 0.7 copy.42
  290.2 0.0 all-gather.14.cloned.1.call-start
  290.3 0.5 all-gather.14.cloned.1.call-update
  290.8 0.0 reduce-scatter.2.cloned.1.call-start
  290.9 0.1 select_reduce_fusion.1
  291.0 0.1 select_reduce_fusion
  291.1 0.2 broadcast_compare_fusion
  291.3 0.1 slice.36
  291.4 25.1 %all-gather.12.cloned.1.call-done = bf16[1024,2,2,128]{3,0,2,1:T(8,128)(2,1)} async-done(((bf16[256,2,2,128]{3,0,2,1:T(8,128)(2,1)}), bf16[1024,2,2,128]{3,0,2,1:T(8,128)(2,1)}) %all-gather.12.cloned.1.call-update) | async-done | bytes 1048592 | tf_op jit(solution)/shard_map/all_gather | solution.py:109
  316.5 1.8 fusion.15
  318.3 0.8 fusion.16
  319.1 0.8 fusion.22
  319.9 43.5 %all-gather.14.cloned.1.call-done = bf16[256,4096]{1,0:T(8,128)(2,1)} async-done(((bf16[256,1024]{1,0:T(8,128)(2,1)}), bf16[256,4096]{1,0:T(8,128)(2,1)}) %all-gather.14.cloned.1.call-update) | async-done | bytes 2097168 | tf_op jit(solution)/shard_map/all_gather | solution.py:137
  363.3 3.6 convolution_convert_fusion
  367.0 40.1 %reduce-scatter.2.cloned.1.call-done = bf16[256,512]{1,0:T(8,128)(2,1)} async-done(((bf16[256,4096]{1,0:T(8,128)(2,1)}), bf16[256,512]{1,0:T(8,128)(2,1)}) %reduce-scatter.2.cloned.1.call-update) | async-done | bytes 262160 | tf_op jit(solution)/shard_map/reduce_scatter | solution.py:140
  407.1 1.8 add_convert_fusion
  (34 shorter events, 0.3 us)
Async XLA Ops:
  6.5 5.8 %copy-start.3 = (s32[4,2]{0,1:T(2,128)S(1)}, s32[4,2]{0,1:T(2,128)}, u32[]{:S(2)}) copy-start(s32[4,2]{0,1:T(2,128)} %param.18) | copy-start | bytes 100
  6.5 6.4 %copy-start.5 = (s32[4]{0:T(128)S(1)}, s32[4]{0:T(128)}, u32[]{:S(2)}) copy-start(s32[4]{0:T(128)} %param.17) | copy-start | bytes 52
  6.5 6.4 %copy-start = (bf16[256,4096]{1,0:T(8,128)(2,1)S(1)}, bf16[256,4096]{1,0:T(8,128)(2,1)}, u32[]{:S(2)}) copy-start(bf16[256,4096]{1,0:T(8,128)(2,1)} %param.10) | copy-start | bytes 6291460
  6.5 51.1 %all-gather.6.cloned.1.call-start = ((), (), s32[]{:S(2)}) async-start(), calls=%async_computation.2 | async-start | bytes 2621440 | tf_op jit(solution)/shard_map/all_gather | solution.py:54
  7.3 6.2 %copy-start.1 = (f32[2,4096]{1,0:T(2,128)S(1)}, f32[2,4096]{1,0:T(2,128)}, u32[]{:S(2)}) copy-start(f32[2,4096]{1,0:T(2,128)} %param.11) | copy-start | bytes 98308
  7.3 15.9 %all-to-all-start = ((bf16[4,3,64,512]{3,2,1,0:T(8,128)(2,1)}), bf16[4,3,64,512]{3,2,1,0:T(8,128)(2,1)S(1)}, u32[]{:S(2)}, u32[]{:S(2)}) async-start(bf16[4,3,64,512]{3,2,1,0:T(8,128)(2,1)} %bitcast.71), calls=%async_computation | async-start | bytes 1572864 | tf_op jit(solution)/shard_map/all_to_all | solution.py:57
  11.5 92.3 %all-gather.8.cloned.1.call-start = ((), (), s32[]{:S(2)}) async-start(), calls=%async_computation.3 | async-start | bytes 2621440 | tf_op jit(solution)/shard_map/all_gather | solution.py:91
  12.3 155.6 %all-reduce.2.cloned.1.call-start = ((), (), s32[]{:S(2)}) async-start(), calls=%async_computation.4 | async-start | bytes 4194304 | tf_op jit(solution)/shard_map/psum | solution.py:94
  107.5 176.3 %all-gather.10.cloned.1.call-start = ((), (), s32[]{:S(2)}) async-start(), calls=%async_computation.5 | async-start | bytes 7864320 | tf_op jit(solution)/shard_map/all_gather | solution.py:98
  110.2 206.3 %all-gather.12.cloned.1.call-start = ((), (), s32[]{:S(2)}) async-start(), calls=%async_computation.6 | async-start | bytes 1310720 | tf_op jit(solution)/shard_map/all_gather | solution.py:109
  289.1 1.7 copy-start.2
  290.2 73.1 %all-gather.14.cloned.1.call-start = ((), (), s32[]{:S(2)}) async-start(), calls=%async_computation.7 | async-start | bytes 2621440 | tf_op jit(solution)/shard_map/all_gather | solution.py:137
  290.8 116.3 %reduce-scatter.2.cloned.1.call-start = ((), (), s32[]{:S(2)}) async-start(), calls=%async_computation.8 | async-start | bytes 2359296 | tf_op jit(solution)/shard_map/reduce_scatter | solution.py:140
  316.5 2.6 copy-start.4
Sparse Core Ops, SparseCore 0:
  8.9 48.6 all-gather.5
  59.2 44.6 all-gather.7
  107.7 60.1 all-reduce.1
  169.3 114.5 all-gather.9
  290.3 26.1 all-gather.11
  317.9 45.3 all-gather.13
  367.1 39.9 reduce-scatter.1
where the time goes:
time: 416 us
  waiting for transfers between devices  366 us (88%)
  matrix products  18.1 us (4%)
  between operations  13.7 us (3%)
  other arithmetic  8.08 us (2%)
  local copies, waits for them, and re-layouts  4.98 us (1%)
  starting transfers between devices  4.45 us (1%)
    all_gather x1, waiting for transfers between devices, per_device(): shard_piece = lax.all_gather(w_self_qkv, 'ctx', axis=0, tiled=True)  112 us
    psum x1, waiting for transfers between devices, per_device(): lax.psum(cross_term.astype(jnp.bfloat16), ('enc', 'mp')).astype(jnp.float32)  57.6 us
    all_gather x1, waiting for transfers between devices, per_device(): lax.all_gather(w_self_out, 'ctx', axis=1, tiled=True)  43.5 us
    all_gather x1, waiting for transfers between devices, per_device(): lax.all_gather(w_cross_out, 'ctx', axis=1, tiled=True)  42.9 us
    reduce_scatter x1, waiting for transfers between devices, per_device(): lax.psum_scatter(self_term.astype(jnp.bfloat16), ('enc', 'mp'), scatter_d...  40.1 us
    all_gather x1, waiting for transfers between devices, per_device(): lax.all_gather(w_cross_query, 'ctx', axis=0, tiled=True)  33.6 us
    all_gather x1, waiting for transfers between devices, per_device(): shard_piece = lax.all_gather(keys_values, 'ctx', axis=0, tiled=True)  25.1 us
    all_to_all x1, waiting for transfers between devices, per_device(): lax.all_to_all(nbr_kv[0, 0], 'enc', split_axis=0, concat_axis=0, tiled=True)  9.64 us
  transfers between devices with their start and end apart: 8, of which 8 were waited for; matrix products, arithmetic and copies ran while one was open for 4% of the time, Pallas kernels for 0%

commit v1 on v0

--- a/solution.py
+++ b/solution.py
@@ -1,9 +1,17 @@
+import functools
 import math
 
 import jax
 import jax.numpy as jnp
 from jax import lax
+from jax.experimental import pallas as pl
+from jax.experimental.pallas import tpu as pltpu
 from jax.sharding import PartitionSpec as P
+
+MESH = pl.DeviceIdType.MESH
+VMEM_GRANT = 56 * 1024 * 1024
+BF16 = jnp.bfloat16
+F32 = jnp.float32
 
 HD = 128
 SPAN = 64
@@ -143,6 +151,370 @@
     return (mid_share.astype(jnp.float32) + out_share).astype(jnp.bfloat16)
 
 
+def dot(a, b):
+    return jnp.dot(a, b, preferred_element_type=F32)
+
+
+def dot_t(a, b):
+    return lax.dot_general(a, b, (((1,), (1,)), ((), ())), preferred_element_type=F32)
+
+
+def block_kernel(
+    hid, gains, wq, wco, wqkv, wso, nbr, cnt, nsrc, order, out,
+    hid_all, nbr_all, qsend, qpart, rs0, att_all, wso_all, term, corebuf, cs, rsbuf, mid_all,
+    sssend, sspart, qkvsend, qkvpart, qbuf, kv_all, midown, att2, fother, fmine, fcore, fsum, frs,
+    send_sems, recv_sems,
+):
+    c, e, m = lax.axis_index("ctx"), lax.axis_index("enc"), lax.axis_index("mp")
+    n = hid_all.shape[0]
+    tok, width = hid.shape
+    shard = width // n
+    feats = wq.shape[1]
+    heads = feats // HD
+    slots = nbr.shape[1]
+    n_enc = nbr.shape[0]
+    rows = tok // 8
+    half = tok // 2
+    cols = out.shape[1]
+    attn_scale = 1.0 / math.sqrt(HD)
+
+    core, y = lax.rem(e, 2), e // 2
+    mate = {"enc": e + 1 - 2 * core}
+    place = y * 2 + m
+
+    def at_place(p):
+        y2 = 1 - y if p & 2 else y
+        m2 = 1 - m if p & 1 else m
+        return y2, m2
+
+    def peer(p):
+        y2, m2 = at_place(p)
+        return {"enc": y2 * 2 + core, "mp": m2}
+
+    def ctx_of(k):
+        return lax.rem(c + k, n)
+
+    def src_of(k):
+        return lax.rem(c - k + n, n)
+
+    issued = []
+
+    def rcopy(src, dst, device, recv=None, start=True):
+        i = rcopy.count
+        rcopy.count += 1
+        d = pltpu.make_async_remote_copy(
+            src_ref=src, dst_ref=dst, send_sem=send_sems.at[i],
+            recv_sem=recv_sems.at[i if recv is None else recv],
+            device_id=device, device_id_type=MESH,
+        )
+        if start:
+            d.start()
+            issued.append(d)
+        return d
+
+    rcopy.count = 0
+
+    barrier = pltpu.get_barrier_semaphore()
+    friends = [{"ctx": ctx_of(k)} for k in range(1, n)]
+    friends += [{"enc": lax.rem(e + k, n_enc)} for k in range(1, n_enc)]
+    friends += [peer(1), peer(3)]
+    for f in friends:
+        pl.semaphore_signal(barrier, inc=1, device_id=f, device_id_type=MESH)
+    pl.semaphore_wait(barrier, len(friends))
+
+    my_rows = pl.ds(pl.multiple_of(core * half + place * rows, rows), rows)
+    my_half = pl.ds(pl.multiple_of(core * half, half), half)
+    mate_half = pl.ds(pl.multiple_of((1 - core) * half, half), half)
+    my_shard = pl.ds(pl.multiple_of(c * shard, shard), shard)
+
+    a1 = {}
+    for k in range(1, n):
+        t = ctx_of(k)
+        there = pl.ds(pl.multiple_of(t * shard, shard), shard)
+        a1[k] = rcopy(hid.at[my_rows, there], hid_all.at[c, my_rows, :], {"ctx": t})
+    nb = []
+    for k in range(1, n_enc):
+        f = lax.rem(e + k, n_enc)
+        nb.append(rcopy(nbr.at[f], nbr_all.at[pl.ds(e * slots, slots)], {"enc": f}))
+    hid_all[c] = hid[:, my_shard]
+    nbr_all[pl.ds(e * slots, slots)] = nbr[e]
+    gain0 = gains[0:1, my_shard]
+    gain1 = gains[1:2, my_shard]
+
+    def project_query(s):
+        x = (hid_all[s].astype(F32) * gain0).astype(BF16)
+        qsend[s] = dot(x, wq[...]).astype(BF16)
+
+    a2 = {}
+    for k in range(1, n):
+        s = src_of(k)
+        a1[k].wait_recv()
+        for p in (3, 1, 2):
+            block = hid_all.at[s, my_rows, :]
+            a2[k, p] = rcopy(block, block, peer(p))
+    project_query(c)
+    squares = jnp.zeros((tok, 1), F32)
+    for j in range(n):
+        x = hid[:, j * shard:(j + 1) * shard].astype(F32)
+        squares = squares + jnp.sum(x * x, axis=1, keepdims=True)
+    rs0[...] = jnp.broadcast_to(lax.rsqrt(squares / width + epsilon), rs0.shape)
+    a3 = {}
+    for k in range(1, n):
+        s = src_of(k)
+        for p in (1, 2, 3):
+            a2[k, p].wait_recv()
+        block = hid_all.at[s, my_half, :]
+        a3[k] = rcopy(block, block, mate)
+    qs = []
+    for k in range(1, n):
+        s = src_of(k)
+        a3[k].wait_recv()
+        project_query(s)
+        qs.append(rcopy(qsend.at[s], qpart.at[k - 1], {"ctx": s}))
+    for d in nb:
+        d.wait_recv()
+    for d in qs:
+        d.wait_recv()
+    q = qsend[c].astype(F32)
+    for k in range(n - 1):
+        q = q + qpart[k].astype(F32)
+    q = (q * rs0[:, 0:1]).astype(BF16)
+
+    spans, per_span = nsrc.shape
+    lane = lax.broadcasted_iota(jnp.int32, (SPAN, per_span * SPAN), 1)
+    for i in range(spans):
+        kv = []
+        for j in range(per_span):
+            chosen = nsrc[i, j]
+            rank = 0
+            for i2 in range(i):
+                for j2 in range(per_span):
+                    rank = rank + jnp.where(nsrc[i2, j2] == chosen, 1, 0)
+            kv.append(nbr_all[chosen * slots + rank])
+        alive = lane < cnt[i] * SPAN
+        for u in range(heads):
+            lo = 2 * u * HD
+            keys = jnp.concatenate([b[:, lo:lo + HD] for b in kv], axis=0)
+            values = jnp.concatenate([b[:, lo + HD:lo + 2 * HD] for b in kv], axis=0)
+            qi = q[i * SPAN:(i + 1) * SPAN, u * HD:(u + 1) * HD]
+            sc = jnp.where(alive, dot_t(qi, keys) * attn_scale, far_below)
+            w = jnp.exp(sc - jnp.max(sc, axis=1, keepdims=True))
+            mixed = dot(w.astype(BF16), values) / jnp.sum(w, axis=1, keepdims=True)
+            att_all[c, i * SPAN:(i + 1) * SPAN, u * HD:(u + 1) * HD] = mixed.astype(BF16)
+
+    at = {k: rcopy(att_all.at[c], att_all.at[c], {"ctx": ctx_of(k)}) for k in range(1, n)}
+    ws = [rcopy(wso, wso_all.at[c], {"ctx": ctx_of(k)}) for k in range(1, n)]
+    wso_all[c] = wso[...]
+
+    c2 = {}
+    for k in range(n):
+        s = src_of(k)
+        if k:
+            at[k].wait_recv()
+        term[s] = dot(att_all[s], wco[...]).astype(BF16)
+        c2[k] = rcopy(term.at[s, mate_half, :], corebuf.at[s], mate)
+    c3 = {}
+    for k in range(n):
+        s = src_of(k)
+        c2[k].wait_recv()
+        cs[s] = (term[s, my_half, :].astype(F32) + corebuf[s].astype(F32)).astype(BF16)
+        for p in (3, 1, 2):
+            y2, m2 = at_place(p)
+            theirs = pl.ds(pl.multiple_of((y2 * 2 + m2) * rows, rows), rows)
+            c3[k, p] = rcopy(cs.at[s, theirs, :], rsbuf.at[p - 1, s], peer(p))
+    c4 = {}
+    for k in range(n):
+        s = src_of(k)
+        total = hid_all[s, my_rows, :].astype(F32)
+        total = total + cs[s, pl.ds(pl.multiple_of(place * rows, rows), rows), :].astype(F32)
+        for p in (1, 2, 3):
+            c3[k, p].wait_recv()
+            total = total + rsbuf[p - 1, s].astype(F32)
+        mid_all[s, my_rows, :] = total.astype(BF16)
+        block = mid_all.at[s, my_rows, :]
+        for p in (3, 1, 2):
+            c4[k, p] = rcopy(block, block, peer(p))
+    c5 = {}
+    for k in range(n):
+        s = src_of(k)
+        for p in (1, 2, 3):
+            c4[k, p].wait_recv()
+        block = mid_all.at[s, my_half, :]
+        c5[k] = rcopy(block, block, mate)
+
+    parts = []
+    for k in list(range(1, n)) + [0]:
+        s = src_of(k)
+        c5[k].wait_recv()
+        x = mid_all[s].astype(F32)
+        squares = jnp.sum(x * x, axis=1, keepdims=True)
+        sssend[s] = jnp.broadcast_to(squares, (tok, HD)).T[0:8]
+        qkvsend[s] = dot((x * gain1).astype(BF16), wqkv[...]).astype(BF16)
+        if k:
+            parts.append(rcopy(qkvsend.at[s], qkvpart.at[k - 1], {"ctx": s}))
+            parts.append(rcopy(sssend.at[s], sspart.at[k - 1], {"ctx": s}))
+
+    my_cols = pl.ds(pl.multiple_of(m * cols, cols), cols)
+    recv = rcopy.count
+    residual = []
+    for k in range(1, n):
+        t = ctx_of(k)
+        residual.append(
+            rcopy(mid_all.at[t, :, my_cols], midown, {"ctx": t}, recv=recv, start=False)
+        )
+
+    @pl.when(c == e)
+    def _():
+        for d in residual:
+            d.start()
+        midown[...] = mid_all[c, :, my_cols]
+
+    for d in parts:
+        d.wait_recv()
+    squares = sssend[c]
+    for k in range(n - 1):
+        squares = squares + sspart[k]
+    squares = jnp.broadcast_to(squares[0:1], (HD, tok)).T[:, 0:1]
+    row_scale = lax.rsqrt(squares / width + epsilon)
+
+    def whole(lo, hi):
+        total = qkvsend[c, :, lo:hi].astype(F32)
+        for k in range(n - 1):
+            total = total + qkvpart[k, :, lo:hi].astype(F32)
+        return (total * row_scale).astype(BF16)
+
+    kv_all[c] = whole(feats, 3 * feats)
+    kvs = {k: rcopy(kv_all.at[c], kv_all.at[c], {"ctx": ctx_of(k)}) for k in range(1, n)}
+    qbuf[...] = whole(0, feats)
+
+    def places(s, shape, axis):
+        index = lax.broadcasted_iota(jnp.int32, shape, axis)
+        first = s * (tok // SPAN)
+        found = jnp.zeros(shape, jnp.int32)
+        for b in range(tok // SPAN):
+            found = jnp.where(index // SPAN == b, order[first + b], found)
+        return found * SPAN + lax.rem(index, SPAN)
+
+    query_places = places(c, (tok, 1), 0)
+    tops = [jnp.full((tok, 1), far_below, F32) for _ in range(heads)]
+    sums = [jnp.zeros((tok, 1), F32) for _ in range(heads)]
+    accs = [jnp.zeros((tok, HD), F32) for _ in range(heads)]
+    for k in range(n):
+        s = src_of(k)
+        if k:
+            kvs[k].wait_recv()
+        visible = places(s, (1, tok), 1) <= query_places
+        for u in range(heads):
+            keys = kv_all[s, :, u * HD:(u + 1) * HD]
+            values = kv_all[s, :, feats + u * HD:feats + (u + 1) * HD]
+            sc = dot_t(qbuf[:, u * HD:(u + 1) * HD], keys) * attn_scale
+            sc = jnp.where(visible, sc, far_below)
+            top = jnp.maximum(tops[u], jnp.max(sc, axis=1, keepdims=True))
+            w = jnp.where(visible, jnp.exp(sc - top), 0.0)
+            shrink = jnp.exp(tops[u] - top)
+            sums[u] = sums[u] * shrink + jnp.sum(w, axis=1, keepdims=True)
+            accs[u] = accs[u] * shrink + dot(w.astype(BF16), values)
+            tops[u] = top
+    for u in range(heads):
+        att2[:, u * HD:(u + 1) * HD] = (accs[u] / sums[u]).astype(BF16)
+
+    for d in ws:
+        d.wait_recv()
+    f1 = {}
+    for p in (3, 1, 2, 0):
+        y2, m2 = at_place(p)
+        there = pl.ds(pl.multiple_of(m2 * cols, cols), cols)
+        fother[p] = dot(att2[...], wso_all[y2 * 2 + 1 - core, :, there]).astype(BF16)
+        f1[p] = rcopy(fother.at[p], fcore.at[p], mate)
+        fmine[p] = dot(att2[...], wso_all[y2 * 2 + core, :, there]).astype(BF16)
+    f2 = {}
+    for p in (3, 1, 2):
+        f1[p].wait_recv()
+        fsum[p - 1] = (fmine[p].astype(F32) + fcore[p].astype(F32)).astype(BF16)
+        f2[p] = rcopy(fsum.at[p - 1], frs.at[p - 1], peer(p))
+    f1[0].wait_recv()
+
+    @pl.when(c == e)
+    def _():
+        for d in residual:
+            d.wait_send()
+
+    @pl.when(c != e)
+    def _():
+        residual[0].wait_recv()
+
+    total = midown[...].astype(F32) + fmine[0].astype(F32) + fcore[0].astype(F32)
+    for p in (1, 2, 3):
+        f2[p].wait_recv()
+        total = total + frs[p - 1].astype(F32)
+    out[...] = total.astype(BF16)
+    for d in issued:
+        d.wait_send()
+
+
+def scratch_shapes(n, n_enc, tok, width, feats, slots, nbr_rows, pair_width, cols):
+    shard = width // n
+    half, rows = tok // 2, tok // 8
+    return [
+        ((n, tok, shard), BF16),
+        ((n_enc * slots, nbr_rows, pair_width), BF16),
+        ((n, tok, feats), BF16),
+        ((n - 1, tok, feats), BF16),
+        ((tok, HD), F32),
+        ((n, tok, feats), BF16),
+        ((n, feats, shard), BF16),
+        ((n, tok, shard), BF16),
+        ((n, half, shard), BF16),
+        ((n, half, shard), BF16),
+        ((3, n, rows, shard), BF16),
+        ((n, tok, shard), BF16),
+        ((n, 8, tok), F32),
+        ((n - 1, 8, tok), F32),
+        ((n, tok, 3 * feats), BF16),
+        ((n - 1, tok, 3 * feats), BF16),
+        ((tok, feats), BF16),
+        ((n, tok, 2 * feats), BF16),
+        ((tok, cols), BF16),
+        ((tok, feats), BF16),
+        ((4, tok, cols), BF16),
+        ((4, tok, cols), BF16),
+        ((4, tok, cols), BF16),
+        ((3, tok, cols), BF16),
+        ((3, tok, cols), BF16),
+    ]
+
+
+def per_device_any(sizes, *args):
+    n, n_enc, n_mp = sizes
+    hidden_in, norm_gains, w_cross_query, w_cross_out, w_self_qkv, w_self_out, nbr_kv = args[:7]
+    tok, width = hidden_in.shape
+    feats = w_cross_query.shape[1]
+    cols = width // (n_enc * n_mp)
+    slots, nbr_rows, pair_width = nbr_kv.shape[3:]
+    held = scratch_shapes(n, n_enc, tok, width, feats, slots, nbr_rows, pair_width, cols)
+    need = sum(math.prod(shape) * jnp.dtype(kind).itemsize for shape, kind in held)
+    if need > VMEM_GRANT // 2 or (n_enc, n_mp) != (4, 2) or width != n * 2 * cols:
+        return per_device(*args)
+    copies = 96
+    vmem = pl.BlockSpec(memory_space=pltpu.VMEM)
+    smem = pl.BlockSpec(memory_space=pltpu.SMEM)
+    return pl.pallas_call(
+        block_kernel,
+        out_shape=jax.ShapeDtypeStruct((tok, cols), BF16),
+        in_specs=[vmem] * 7 + [smem] * 3,
+        out_specs=vmem,
+        scratch_shapes=[pltpu.VMEM(shape, kind) for shape, kind in held]
+        + [pltpu.SemaphoreType.DMA((copies,)), pltpu.SemaphoreType.DMA((copies,))],
+        compiler_params=pltpu.CompilerParams(
+            collective_id=0, has_side_effects=True, vmem_limit_bytes=VMEM_GRANT
+        ),
+    )(
+        hidden_in, norm_gains, w_cross_query, w_cross_out,
+        w_self_qkv.reshape(w_self_qkv.shape[0], 3 * feats), w_self_out,
+        nbr_kv[0, 0], *args[7:],
+    )
+
+
 def solution(mesh):
     in_specs = (
         P("ctx", None),
@@ -157,6 +529,7 @@
         P(),
     )
     out_specs = P("ctx", ("enc", "mp"))
+    sizes = (mesh.shape["ctx"], mesh.shape["enc"], mesh.shape["mp"])
     return jax.shard_map(
-        per_device, mesh=mesh, in_specs=in_specs, out_specs=out_specs, check_vma=False
-    )
+        functools.partial(per_device_any, sizes), mesh=mesh, in_specs=in_specs, out_specs=out_specs, check_vma=False
+    )

time: 416 us -> 191 us (0.46)
  waiting for transfers between devices: 366 us -> 0 us
  Pallas kernels: 0 us -> 183 us
  matrix products: 18.1 us -> 0 us
  between operations: 13.7 us -> 0.03 us
  other arithmetic: 8.08 us -> 0 us
  starting transfers between devices: 4.45 us -> 0 us
    all_gather x5 -> x0, waiting for transfers between devices: 257 us -> none  [the longest x1 112 us: per_device(): shard_piece = lax.all_gather(w_self_qkv, 'ctx', axis=0, tiled=True)]
    pallas_call x0 -> x1, Pallas kernels: none -> 183 us  [per_device_any(): pl.pallas_call(block_kernel, out_shape=jax.ShapeDtypeStruct((tok, cols),...]
    psum x1 -> x0, waiting for transfers between devices: 57.6 us -> none  [per_device(): lax.psum(cross_term.astype(jnp.bfloat16), ('enc', 'mp')).astype(jnp.float32)]
    reduce_scatter x1 -> x0, waiting for transfers between devices: 40.1 us -> none  [per_device(): lax.psum_scatter(self_term.astype(jnp.bfloat16), ('enc', 'mp'), scatter_d...]
    dot_general x7 -> x0, matrix products: 17.8 us -> none  [the longest x1 5.28 us: per_device(): jnp.dot(columns_part, shard_piece.reshape(shard_piece.shape[0], 3 * featu...]
    all_to_all x1 -> x0, waiting for transfers between devices: 9.64 us -> none  [per_device(): lax.all_to_all(nbr_kv[0, 0], 'enc', split_axis=0, concat_axis=0, tiled=True)]
    reduce_sum x7 -> x0, other arithmetic: 5.62 us -> none  [the longest x2 4.38 us: rms_rows(): jnp.mean(values * values, axis=-1, keepdims=True) + epsilon]
    all_to_all x1 -> x0, starting transfers between devices: 4.25 us -> none  [per_device(): lax.all_to_all(nbr_kv[0, 0], 'enc', split_axis=0, concat_axis=0, tiled=True)]
  transfers between devices with their start and end apart: 8 -> 0, of which waited for: 8 -> 0; matrix products, arithmetic and copies ran while one was open for 4% -> 0% of each run, Pallas kernels for 0% -> 0%
where the time goes in v1:
time: 191 us; the launch traced here: 188 us
  Pallas kernels  183 us (96%)
  local copies, waits for them, and re-layouts  5.64 us (3%)
    pallas_call x1, Pallas kernels, per_device_any(): pl.pallas_call(block_kernel, out_shape=jax.ShapeDtypeStruct((tok, cols),...  183 us
    unnamed x5, local copies, waits for them, and re-layouts  4.05 us

profile of v1, /device:TPU:0, one launch (start us, length us, event | category | flops | bytes accessed | tf_op | source)
XLA Modules:
  0.0 188.3 jit_solution(15232875295244798915)
XLA Ops:
  0.0 1.7 copy.13
  1.7 0.0 copy-start
  1.7 1.6 copy.14.wqkv
  3.3 0.0 copy-done
  3.3 0.7 copy.15.nsrc
  4.0 182.6 %shard_map.100 = bf16[256,512]{1,0:T(8,128)(2,1)} custom-call(bf16[256,4096]{1,0:T(8,128)(2,1)} %hid.1, f32[2,4096]{1,0:T(2,128)} %gains.1, bf16[1024,256]{1,0:T(8,128)(2,1)} %wq.1, bf16[256,1024]{1,0:T(8,128)(2,1)} %wco.1, bf16[1024,768]{1,0:T(8,128)(2,1)} %copy.14.wqkv, bf16[256,1024]{1,0:T(8,128)(2,1)} %wso.1, bf16[4,3,64,512]{3,2,1,0:T(8,128)(2,1)} %bitcast.3, ...), custom_call_target="tpu_custom_call" | custom-call | tf_op jit(solution)/shard_map/pallas_call | solution.py:501
  186.6 1.7 copy.17
Async XLA Ops:
  1.7 1.6 copy-start
